TPU v7x, 512 devices: a whole 4x4x16 slice. The times are simulated.
512 devices in a mesh: row: 32 (over y, x, core), col: 16 (over z).
Axes of the slice: x: 4, y: 4, z: 16, core: 2. Of those that a mesh axis runs over, the one named last changes fastest.
Arguments:
- col_samples: float32 [64, 2, 2048, 128], P('row', None, 'col'), may hold values from -6 to 6
- row_samples: float32 [64, 2, 128, 2048], P('row', None, None, 'col'), may hold values from -6 to 6
- pivot_rows: int32 [64, 128], P('row'), may hold values from 0 to 2047
- rank_blocks: int32 [64], P('row'), may hold values from 1 to 8
- upper_inverse: float32 [2, 2048, 2048], P(None, 'col', 'row'), as said below
- upanel_left: float32 [16, 2, 2048, 128], P('col'), may hold values from -0.125 to 0.125
Outputs:
- panel_right: float32 [64, 2, 128, 2048], P('row', None, None, 'col')
- cores: float32 [64, 16, 2, 128, 128], P('row', 'col')
Inputs may be any that keep to these rules, and one draw needn't show every extreme that they name: `rank_blocks`: the tile's rank is 16 times this. `upper_inverse`: zero below the diagonal in both parts.
All inputs are finite; a program needn't handle non-finite values.
Results may differ from a plain program's by a relative error of at most 0.00007.
Values sent between devices are 32-bit elements; how exact they have to be, the bound alone decides.
No kernel may reach another device: no remote copies, remote signals or barrier semaphores. Data moves between devices by JAX's collectives and lax.ppermute only.
A program may use at most 64 MiB of HBM per device.

v0:
```python
import jax
import jax.numpy as jnp
from jax import lax
from jax.sharding import PartitionSpec as P

RANK_STEP = 16


def complex_product(pattern, left_real, left_imag, right_real, right_imag):

    def single(left, right):
        return jnp.einsum(
            pattern,
            left,
            right,
            precision=lax.Precision.HIGHEST,
            preferred_element_type=jnp.float32,
        )

    real_part = single(left_real, right_real) - single(left_imag, right_imag)
    imag_part = single(left_real, right_imag) + single(left_imag, right_real)
    return (real_part, imag_part)


def scale_rows(values, weight_real, weight_imag):
    wr = weight_real[:, :, None]
    wi = weight_imag[:, :, None]
    real_part = values[:, 0] * wr - values[:, 1] * wi
    imag_part = values[:, 0] * wi + values[:, 1] * wr
    return jnp.stack((real_part, imag_part), axis=1)


def on_device(col_samples, row_samples, pivot_rows, rank_blocks, upper_inverse, upanel_left):
    width_local = col_samples.shape[2]
    ranks_max = row_samples.shape[2]
    offset = lax.axis_index("col") * width_local
    positions = offset + lax.broadcasted_iota(jnp.int32, (1, 1, width_local), 2)
    hits = (pivot_rows[:, :, None] == positions).astype(jnp.float32)
    flipped = jnp.swapaxes(col_samples, 2, 3)
    partial_entries = jnp.sum(flipped * hits[:, None], axis=3)
    entries = lax.psum(partial_entries, "col")
    levels = lax.broadcasted_iota(jnp.int32, (1, ranks_max), 1)
    keeping = (levels < RANK_STEP * rank_blocks[:, None]).astype(jnp.float32)
    magnitude = jnp.maximum(entries[:, 0] * entries[:, 0] + entries[:, 1] * entries[:, 1], 1.0)
    factor_real = keeping * entries[:, 0] / magnitude
    factor_imag = -keeping * entries[:, 1] / magnitude
    scaled = scale_rows(row_samples, factor_real, factor_imag)
    portion = lax.all_gather(upper_inverse, "row", axis=2, tiled=True)
    real_part, imag_part = complex_product(
        "trk,kn->trn", scaled[:, 0], scaled[:, 1], portion[0], portion[1]
    )
    partial_panel = jnp.stack((real_part, imag_part), axis=1)
    panel_local = lax.psum_scatter(partial_panel, "col", scatter_dimension=3, tiled=True)
    portion = lax.all_gather(panel_local, "col", axis=3, tiled=True)
    core_real, core_imag = complex_product(
        "trn,jns->tjrs", portion[:, 0], portion[:, 1], upanel_left[:, 0], upanel_left[:, 1]
    )
    cores = jnp.stack((core_real, core_imag), axis=2)
    return (panel_local, cores)


def solution(mesh):
    in_specs = (
        P("row", None, "col", None),
        P("row", None, None, "col"),
        P("row", None),
        P("row"),
        P(None, "col", "row"),
        P("col", None, None, None),
    )
    out_specs = (P("row", None, None, "col"), P("row", "col", None, None, None))
    return jax.shard_map(
        on_device, mesh=mesh, in_specs=in_specs, out_specs=out_specs, check_vma=False
    )
```

profile of v0, /device:TPU:2, one launch (start us, length us, event | category | flops | bytes accessed | tf_op | source)
XLA Modules:
  0.0 281.9 jit_solution(7301261295972462733)
XLA Ops:
  7.2 0.0 all-gather.3.cloned.1.call-start
  7.2 1.5 copy.12
  8.7 0.0 all-gather.3.cloned.1.call-update
  8.8 0.0 reduce-scatter.2.cloned.1.call-start
  8.8 0.8 compare_convert_fusion
  9.6 1.0 fusion.18
  10.6 36.5 %psum.7 = f32[2,2,128]{2,1,0:T(2,128)S(1)} all-reduce(f32[2,2,128]{2,1,0:T(2,128)S(1)} %fusion.18), channel_id=1, replica_groups=mesh['row'=32,'col'=16] {'col'}, use_global_device_ids=true, to_apply=%region_1.0 | all-reduce | flops 512 | bytes 4096 | tf_op jit(solution)/shard_map/psum | solution.py:41
  47.1 0.7 broadcast_multiply_fusion
  47.8 0.1 select_divide_fusion
  47.8 0.0 copy-start.2
  47.8 27.1 %all-gather.3.cloned.1.call-done = f32[2,128,2048]{1,0,2:T(2,128)} async-done(((f32[2,128,64]{1,0,2:T(2,128)}), f32[2,128,2048]{1,0,2:T(2,128)}) %all-gather.3.cloned.1.call-update) | async-done | bytes 2097168 | tf_op jit(solution)/shard_map/all_gather | solution.py:48
  74.9 4.0 %fusion.25 = (f32[1,128,2048]{1,0,2:T(1,128)S(1)}, f32[1,128,2048]{1,0,2:T(1,128)S(1)}) fusion(f32[2,128,2048]{1,0,2:T(2,128)} %all-gather.3.cloned.1.call-done), kind=kLoop, calls=%fused_computation.41 | loop fusion | bytes 4194304 | tf_op jit(solution)/shard_map/slice | solution.py:50
  78.9 0.0 copy-done.2
  78.9 1.8 fusion.21
  80.8 1.8 fusion.23
  82.6 1.9 fusion
  84.5 1.9 fusion.1
  86.4 2.2 pad_maximum_fusion
  88.6 0.0 copy-start.1
  88.6 0.0 reduce-scatter.2.cloned.1.call-update
  88.7 0.2 all-gather.5.cloned.1.call-start
  88.9 79.6 %reduce-scatter.2.cloned.1.call-done = f32[2,2,128,128]{3,2,0,1:T(8,128)} async-done(((f32[2,2,128,2048]{3,2,0,1:T(8,128)}), f32[2,2,128,128]{3,2,0,1:T(8,128)}) %reduce-scatter.2.cloned.1.call-update) | async-done | bytes 262160 | tf_op jit(solution)/shard_map/reduce_scatter | solution.py:53
  168.5 0.0 all-gather.5.cloned.1.call-update
  168.5 1.7 copy.15
  170.2 93.8 %all-gather.5.cloned.1.call-done = f32[2,2,128,2048]{3,2,0,1:T(8,128)} async-done(((f32[2,2,128,128]{3,2,0,1:T(8,128)}), f32[2,2,128,2048]{3,2,0,1:T(8,128)}) %all-gather.5.cloned.1.call-update) | async-done | bytes 4194320 | tf_op jit(solution)/shard_map/all_gather | solution.py:54
  263.9 0.0 copy-done.1
  263.9 0.0 copy-start
  263.9 3.6 %fusion.2 = f32[2,128,128]{2,1,0:T(8,128)S(1)} fusion(f32[2,2,128,2048]{3,2,0,1:T(8,128)} %all-gather.5.cloned.1.call-done, f32[1,2,2048,128]{3,2,1,0:T(8,128)S(1)} %copy-done.1), kind=kOutput, calls=%fused_computation.7 | convolution fusion | flops 805306368 | bytes 3276800 | tf_op jit(solution)/shard_map/trn,jns->tjrs/dot_general | solution.py:12
  267.5 3.4 %fusion.3 = f32[2,128,128]{2,1,0:T(8,128)S(1)} fusion(f32[2,2,128,2048]{3,2,0,1:T(8,128)} %all-gather.5.cloned.1.call-done, f32[1,2,2048,128]{3,2,1,0:T(8,128)S(1)} %copy-done.1), kind=kOutput, calls=%fused_computation.8 | convolution fusion | flops 805306368 | bytes 3276800 | tf_op jit(solution)/shard_map/trn,jns->tjrs/dot_general | solution.py:12
  270.9 0.0 copy-done
  270.9 1.8 fusion.9
  272.8 1.8 fusion.7
  274.6 0.7 copy.16
  (3 shorter events, 0.0 us)
Async XLA Ops:
  7.2 67.7 %all-gather.3.cloned.1.call-start = ((), (), s32[]{:S(2)}) async-start(), calls=%async_computation.1 | async-start | bytes 2162688 | tf_op jit(solution)/shard_map/all_gather | solution.py:48
  8.8 159.7 %reduce-scatter.2.cloned.1.call-start = ((), (), s32[]{:S(2)}) async-start(), calls=%async_computation.2 | async-start | bytes 4456448 | tf_op jit(solution)/shard_map/reduce_scatter | solution.py:53
  47.8 31.1 %copy-start.2 = (f32[2,2,128,128]{3,2,1,0:T(8,128)S(1)}, f32[2,2,128,128]{3,2,1,0:T(8,128)}, u32[]{:S(2)}) copy-start(f32[2,2,128,128]{3,2,1,0:T(8,128)} %param.7) | copy-start | bytes 786436
  88.6 175.3 %copy-start.1 = (f32[1,2,2048,128]{3,2,1,0:T(8,128)S(1)}, f32[1,2,2048,128]{3,2,1,0:T(8,128)}, u32[]{:S(2)}) copy-start(f32[1,2,2048,128]{3,2,1,0:T(8,128)} %param.11) | copy-start | bytes 6291460
  88.7 175.3 %all-gather.5.cloned.1.call-start = ((), (), s32[]{:S(2)}) async-start(), calls=%async_computation.3 | async-start | bytes 4456448 | tf_op jit(solution)/shard_map/all_gather | solution.py:54
  263.9 7.0 %copy-start = (f32[2,2,128,2048]{3,2,0,1:T(8,128)S(1)}, f32[2,2,128,2048]{3,2,0,1:T(8,128)}, u32[]{:S(2)}) copy-start(f32[2,2,128,2048]{3,2,0,1:T(8,128)} %all-gather.5.cloned.1.call-done) | copy-start | bytes 12582916
Sparse Core Ops, SparseCore 0:
  11.7 63.1 all-gather.2
  88.8 79.6 reduce-scatter.1
  170.5 93.4 all-gather.4
where the time goes:
time: 282 us
  waiting for transfers between devices  200 us (71%)
  blocking collectives  36.5 us (13%)
  matrix products  18.1 us (6%)
  between operations  13.9 us (5%)
  local copies, waits for them, and re-layouts  7.92 us (3%)
  other arithmetic  4.73 us (2%)
    all_gather x1, waiting for transfers between devices, on_device(): portion = lax.all_gather(panel_local, 'col', axis=3, tiled=True)  93.8 us
    reduce_scatter x1, waiting for transfers between devices, on_device(): lax.psum_scatter(partial_panel, 'col', scatter_dimension=3, tiled=True)  79.6 us
    psum x1, blocking collectives, on_device(): entries = lax.psum(partial_entries, 'col')  36.5 us
    all_gather x1, waiting for transfers between devices, on_device(): portion = lax.all_gather(upper_inverse, 'row', axis=2, tiled=True)  27.1 us
    dot_general x8, matrix products, single(): jnp.einsum(pattern, left, right, precision=lax.Precision.HIGHEST, preferr...  18.1 us
  transfers between devices with their start and end apart: 3, of which 3 were waited for; matrix products, arithmetic and copies ran while one was open for 1% of the time, Pallas kernels for 0%

commit v1 on v0

--- a/solution.py
+++ b/solution.py
@@ -51,7 +51,26 @@
     )
     partial_panel = jnp.stack((real_part, imag_part), axis=1)
     panel_local = lax.psum_scatter(partial_panel, "col", scatter_dimension=3, tiled=True)
-    portion = lax.all_gather(panel_local, "col", axis=3, tiled=True)
+    size, here, width = (lax.axis_size("col"), lax.axis_index("col"), panel_local.shape[3])
+    right_2 = [(i, (i + 1) % size) for i in range(size)]
+    left_2 = [(i, (i - 1) % size) for i in range(size)]
+    result = jnp.zeros(
+        (*panel_local.shape[:3], size * width, *panel_local.shape[3 + 1 :]), panel_local.dtype
+    )
+    result = lax.dynamic_update_slice_in_dim(result, panel_local, here * width, axis=3)
+    from_left = from_right = panel_local
+    half = size // 2
+    for hop in range(1, half + 1):
+        from_left = lax.ppermute(from_left, "col", right_2)
+        result = lax.dynamic_update_slice_in_dim(
+            result, from_left, (here - hop) % size * width, axis=3
+        )
+        if hop < size - half:
+            from_right = lax.ppermute(from_right, "col", left_2)
+            result = lax.dynamic_update_slice_in_dim(
+                result, from_right, (here + hop) % size * width, axis=3
+            )
+    portion = result
     core_real, core_imag = complex_product(
         "trn,jns->tjrs", portion[:, 0], portion[:, 1], upanel_left[:, 0], upanel_left[:, 1]
     )

time: 282 us -> 264 us (0.936)
  the two profiles are of different devices: /device:TPU:2 before, /device:TPU:6 now
where the time goes in v1:
time: 264 us
  waiting for transfers between devices  132 us (50%)
  starting transfers between devices  52.5 us (20%)
  blocking collectives  36.5 us (14%)
  matrix products  14.8 us (6%)
  between operations  14.7 us (6%)
  local copies, waits for them, and re-layouts  8.02 us (3%)
  other arithmetic  4.74 us (2%)
    reduce_scatter x1, waiting for transfers between devices, on_device(): lax.psum_scatter(partial_panel, 'col', scatter_dimension=3, tiled=True)  80.4 us
    psum x1, blocking collectives, on_device(): entries = lax.psum(partial_entries, 'col')  36.5 us
    ppermute x7, starting transfers between devices, on_device(): from_right = lax.ppermute(from_right, 'col', left_2)  36.4 us
    all_gather x1, waiting for transfers between devices, on_device(): portion = lax.all_gather(upper_inverse, 'row', axis=2, tiled=True)  27 us
    ppermute x8, waiting for transfers between devices, on_device(): from_left = lax.ppermute(from_left, 'col', right_2)  23.2 us
    ppermute x8, starting transfers between devices, on_device(): from_left = lax.ppermute(from_left, 'col', right_2)  16.1 us
    dot_general x8, matrix products, single(): jnp.einsum(pattern, left, right, precision=lax.Precision.HIGHEST, preferr...  14.8 us
  transfers between devices with their start and end apart: 17, of which 12 were waited for; matrix products, arithmetic and copies ran while one was open for 2% of the time, Pallas kernels for 0%

profile of v1, /device:TPU:6, one launch (start us, length us, event | category | flops | bytes accessed | tf_op | source)
XLA Modules:
  0.0 263.7 jit_solution(9033981773858250884)
XLA Ops:
  7.2 0.0 all-gather.2.cloned.1.call-start
  7.2 1.6 copy.12
  8.8 0.0 reduce-scatter.2.cloned.1.call-start
  8.9 0.8 compare_convert_fusion
  9.6 1.0 fusion.18
  10.6 36.5 %psum.7 = f32[2,2,128]{2,1,0:T(2,128)S(1)} all-reduce(f32[2,2,128]{2,1,0:T(2,128)S(1)} %fusion.18), channel_id=1, replica_groups=mesh['row'=32,'col'=16] {'col'}, use_global_device_ids=true, to_apply=%region_1.0 | all-reduce | flops 512 | bytes 4096 | tf_op jit(solution)/shard_map/psum | solution.py:41
  47.1 0.7 broadcast_multiply_fusion
  47.8 0.1 select_divide_fusion
  47.9 27.0 %all-gather.2.cloned.1.call-done = f32[2,128,2048]{1,0,2:T(2,128)} async-done(((f32[2,128,64]{1,0,2:T(2,128)}), f32[2,128,2048]{1,0,2:T(2,128)}) %all-gather.2.cloned.1.call-update) | async-done | bytes 2097168 | tf_op jit(solution)/shard_map/all_gather | solution.py:48
  74.9 4.1 %fusion.25 = (f32[1,128,2048]{1,0,2:T(1,128)S(1)}, f32[1,128,2048]{1,0,2:T(1,128)S(1)}) fusion(f32[2,128,2048]{1,0,2:T(2,128)} %all-gather.2.cloned.1.call-done), kind=kLoop, calls=%fused_computation.57 | loop fusion | bytes 4194304 | tf_op jit(solution)/shard_map/slice | solution.py:50
  78.9 1.8 fusion.23
  80.8 1.8 fusion.21
  82.6 1.9 fusion.1
  84.5 1.9 fusion
  86.4 2.2 pad_maximum_fusion
  88.7 80.4 %reduce-scatter.2.cloned.1.call-done = f32[2,2,128,128]{3,2,0,1:T(8,128)} async-done(((f32[2,2,128,2048]{3,2,0,1:T(8,128)}), f32[2,2,128,128]{3,2,0,1:T(8,128)}) %reduce-scatter.2.cloned.1.call-update) | async-done | bytes 262160 | tf_op jit(solution)/shard_map/reduce_scatter | solution.py:53
  169.1 2.5 collective-permute-start
  171.6 4.7 %collective-permute-start.1 = (f32[2,2,128,128]{3,2,0,1:T(8,128)}, f32[2,2,128,128]{3,2,0,1:T(8,128)S(1)}, u32[]{:S(2)}, u32[]{:S(2)}) collective-permute-start(f32[2,2,128,128]{3,2,0,1:T(8,128)} %reduce-scatter.2.cloned.1.call-done), channel_id=1, source_target_pairs={{0,15},{1,0},{2,1},{3,2},{4,3},{5,4},{6,5},{7,6},{8,7},{9,8},{10,9... | collective-permute-start | bytes 786440 | tf_op jit(solution)/shard_map/ppermute | solution.py:69
  176.3 3.4 %collective-permute-done = f32[2,2,128,128]{3,2,0,1:T(8,128)S(1)} collective-permute-done((f32[2,2,128,128]{3,2,0,1:T(8,128)}, f32[2,2,128,128]{3,2,0,1:T(8,128)S(1)}, u32[]{:S(2)}, u32[]{:S(2)}) %collective-permute-start) | collective-permute-done | bytes 262176 | tf_op jit(solution)/shard_map/ppermute | solution.py:64
  179.7 1.9 collective-permute-start.2
  181.6 5.1 %collective-permute-start.3 = (f32[2,2,128,128]{3,2,0,1:T(8,128)S(1)}, f32[2,2,128,128]{3,2,0,1:T(8,128)S(1)}, u32[]{:S(2)}, u32[]{:S(2)}) collective-permute-start(f32[2,2,128,128]{3,2,0,1:T(8,128)S(1)} %collective-permute-done.1), channel_id=1, source_target_pairs={{0,15},{1,0},{2,1},{3,2},{4,3},{5,4},{6,5},{7,6},{8,7},{9,8},{10,9... | collective-permute-start | bytes 786440 | tf_op jit(solution)/shard_map/ppermute | solution.py:69
  186.7 2.4 collective-permute-done.2
  189.1 1.9 collective-permute-start.4
  191.0 5.1 %collective-permute-start.5 = (f32[2,2,128,128]{3,2,0,1:T(8,128)S(1)}, f32[2,2,128,128]{3,2,0,1:T(8,128)S(1)}, u32[]{:S(2)}, u32[]{:S(2)}) collective-permute-start(f32[2,2,128,128]{3,2,0,1:T(8,128)S(1)} %collective-permute-done.3), channel_id=1, source_target_pairs={{0,15},{1,0},{2,1},{3,2},{4,3},{5,4},{6,5},{7,6},{8,7},{9,8},{10,9... | collective-permute-start | bytes 786440 | tf_op jit(solution)/shard_map/ppermute | solution.py:69
  196.5 2.1 collective-permute-done.4
  198.6 1.9 collective-permute-start.6
  200.5 0.5 broadcast_in_dim.2
  201.1 0.7 copy.15
  201.8 5.1 %collective-permute-start.7 = (f32[2,2,128,128]{3,2,0,1:T(8,128)S(1)}, f32[2,2,128,128]{3,2,0,1:T(8,128)S(1)}, u32[]{:S(2)}, u32[]{:S(2)}) collective-permute-start(f32[2,2,128,128]{3,2,0,1:T(8,128)S(1)} %collective-permute-done.5), channel_id=1, source_target_pairs={{0,15},{1,0},{2,1},{3,2},{4,3},{5,4},{6,5},{7,6},{8,7},{9,8},{10,9... | collective-permute-start | bytes 786440 | tf_op jit(solution)/shard_map/ppermute | solution.py:69
  207.0 1.0 collective-permute-done.6
  208.1 1.9 collective-permute-start.8
  210.0 0.8 collective-permute-done.7
  210.8 5.6 %collective-permute-start.9 = (f32[2,2,128,128]{3,2,0,1:T(8,128)S(1)}, f32[2,2,128,128]{3,2,0,1:T(8,128)S(1)}, u32[]{:S(2)}, u32[]{:S(2)}) collective-permute-start(f32[2,2,128,128]{3,2,0,1:T(8,128)S(1)} %collective-permute-done.7), channel_id=1, source_target_pairs={{0,15},{1,0},{2,1},{3,2},{4,3},{5,4},{6,5},{7,6},{8,7},{9,8},{10,9... | collective-permute-start | bytes 786440 | tf_op jit(solution)/shard_map/ppermute | solution.py:69
  216.5 1.9 collective-permute-done.8
  218.4 1.9 collective-permute-start.10
  220.4 1.0 collective-permute-done.9
  221.4 5.6 %collective-permute-start.11 = (f32[2,2,128,128]{3,2,0,1:T(8,128)S(1)}, f32[2,2,128,128]{3,2,0,1:T(8,128)S(1)}, u32[]{:S(2)}, u32[]{:S(2)}) collective-permute-start(f32[2,2,128,128]{3,2,0,1:T(8,128)S(1)} %collective-permute-done.9), channel_id=1, source_target_pairs={{0,15},{1,0},{2,1},{3,2},{4,3},{5,4},{6,5},{7,6},{8,7},{9,8},{10,9... | collective-permute-start | bytes 786440 | tf_op jit(solution)/shard_map/ppermute | solution.py:69
  227.0 2.8 %collective-permute-done.10 = f32[2,2,128,128]{3,2,0,1:T(8,128)S(1)} collective-permute-done((f32[2,2,128,128]{3,2,0,1:T(8,128)S(1)}, f32[2,2,128,128]{3,2,0,1:T(8,128)S(1)}, u32[]{:S(2)}, u32[]{:S(2)}) %collective-permute-start.10) | collective-permute-done | bytes 262176 | tf_op jit(solution)/shard_map/ppermute | solution.py:64
  229.8 1.9 collective-permute-start.12
  231.8 5.1 %collective-permute-start.13 = (f32[2,2,128,128]{3,2,0,1:T(8,128)S(1)}, f32[2,2,128,128]{3,2,0,1:T(8,128)S(1)}, u32[]{:S(2)}, u32[]{:S(2)}) collective-permute-start(f32[2,2,128,128]{3,2,0,1:T(8,128)S(1)} %collective-permute-done.11), channel_id=1, source_target_pairs={{0,15},{1,0},{2,1},{3,2},{4,3},{5,4},{6,5},{7,6},{8,7},{9,8},{10,9... | collective-permute-start | bytes 786440 | tf_op jit(solution)/shard_map/ppermute | solution.py:69
  237.0 2.3 collective-permute-done.12
  239.3 2.1 collective-permute-start.14
  241.5 7.2 %collective-permute-done.14 = f32[2,2,128,128]{3,2,0,1:T(8,128)S(1)} collective-permute-done((f32[2,2,128,128]{3,2,0,1:T(8,128)S(1)}, f32[2,2,128,128]{3,2,0,1:T(8,128)S(1)}, u32[]{:S(2)}, u32[]{:S(2)}) %collective-permute-start.14) | collective-permute-done | bytes 262176 | tf_op jit(solution)/shard_map/ppermute | solution.py:64
  248.8 1.8 fusion.5
  250.6 1.8 fusion.4
  252.5 1.8 fusion.7
  254.3 1.8 fusion.9
  256.2 0.7 copy.16
  (32 shorter events, 0.5 us)
Async XLA Ops:
  7.2 71.8 %copy-start.1 = (f32[2,2,128,128]{3,2,1,0:T(8,128)S(1)}, f32[2,2,128,128]{3,2,1,0:T(8,128)}, u32[]{:S(2)}) copy-start(f32[2,2,128,128]{3,2,1,0:T(8,128)} %param.7) | copy-start | bytes 786436
  7.2 67.7 %all-gather.2.cloned.1.call-start = ((), (), s32[]{:S(2)}) async-start(), calls=%async_computation.1 | async-start | bytes 2162688 | tf_op jit(solution)/shard_map/all_gather | solution.py:48
  8.8 160.3 %reduce-scatter.2.cloned.1.call-start = ((), (), s32[]{:S(2)}) async-start(), calls=%async_computation.2 | async-start | bytes 4456448 | tf_op jit(solution)/shard_map/reduce_scatter | solution.py:53
  169.1 31.9 %copy-start.2 = (f32[2,2,128,128]{3,2,0,1:T(8,128)S(1)}, f32[2,2,128,128]{3,2,0,1:T(8,128)}, u32[]{:S(2)}) copy-start(f32[2,2,128,128]{3,2,0,1:T(8,128)} %reduce-scatter.2.cloned.1.call-done) | copy-start | bytes 786436
  169.1 10.6 %collective-permute-start = (f32[2,2,128,128]{3,2,0,1:T(8,128)}, f32[2,2,128,128]{3,2,0,1:T(8,128)S(1)}, u32[]{:S(2)}, u32[]{:S(2)}) collective-permute-start(f32[2,2,128,128]{3,2,0,1:T(8,128)} %reduce-scatter.2.cloned.1.call-done), channel_id=1, source_target_pairs={{0,1},{1,2},{2,3},{3,4},{4,5},{5,6},{6,7},{7,8},{8,9},{9,10},{10,1... | collective-permute-start | bytes 786440 | tf_op jit(solution)/shard_map/ppermute | solution.py:64
  171.6 10.0 %collective-permute-start.1 = (f32[2,2,128,128]{3,2,0,1:T(8,128)}, f32[2,2,128,128]{3,2,0,1:T(8,128)S(1)}, u32[]{:S(2)}, u32[]{:S(2)}) collective-permute-start(f32[2,2,128,128]{3,2,0,1:T(8,128)} %reduce-scatter.2.cloned.1.call-done), channel_id=1, source_target_pairs={{0,15},{1,0},{2,1},{3,2},{4,3},{5,4},{6,5},{7,6},{8,7},{9,8},{10,9... | collective-permute-start | bytes 786440 | tf_op jit(solution)/shard_map/ppermute | solution.py:69
  179.7 9.5 %collective-permute-start.2 = (f32[2,2,128,128]{3,2,0,1:T(8,128)S(1)}, f32[2,2,128,128]{3,2,0,1:T(8,128)S(1)}, u32[]{:S(2)}, u32[]{:S(2)}) collective-permute-start(f32[2,2,128,128]{3,2,0,1:T(8,128)S(1)} %collective-permute-done), channel_id=1, source_target_pairs={{0,1},{1,2},{2,3},{3,4},{4,5},{5,6},{6,7},{7,8},{8,9},{9,10},{10,1... | collective-permute-start | bytes 786440 | tf_op jit(solution)/shard_map/ppermute | solution.py:64
  181.6 9.5 %collective-permute-start.3 = (f32[2,2,128,128]{3,2,0,1:T(8,128)S(1)}, f32[2,2,128,128]{3,2,0,1:T(8,128)S(1)}, u32[]{:S(2)}, u32[]{:S(2)}) collective-permute-start(f32[2,2,128,128]{3,2,0,1:T(8,128)S(1)} %collective-permute-done.1), channel_id=1, source_target_pairs={{0,15},{1,0},{2,1},{3,2},{4,3},{5,4},{6,5},{7,6},{8,7},{9,8},{10,9... | collective-permute-start | bytes 786440 | tf_op jit(solution)/shard_map/ppermute | solution.py:69
  189.1 9.5 %collective-permute-start.4 = (f32[2,2,128,128]{3,2,0,1:T(8,128)S(1)}, f32[2,2,128,128]{3,2,0,1:T(8,128)S(1)}, u32[]{:S(2)}, u32[]{:S(2)}) collective-permute-start(f32[2,2,128,128]{3,2,0,1:T(8,128)S(1)} %collective-permute-done.2), channel_id=1, source_target_pairs={{0,1},{1,2},{2,3},{3,4},{4,5},{5,6},{6,7},{7,8},{8,9},{9,10},{10,1... | collective-permute-start | bytes 786440 | tf_op jit(solution)/shard_map/ppermute | solution.py:64
  191.0 10.8 %collective-permute-start.5 = (f32[2,2,128,128]{3,2,0,1:T(8,128)S(1)}, f32[2,2,128,128]{3,2,0,1:T(8,128)S(1)}, u32[]{:S(2)}, u32[]{:S(2)}) collective-permute-start(f32[2,2,128,128]{3,2,0,1:T(8,128)S(1)} %collective-permute-done.3), channel_id=1, source_target_pairs={{0,15},{1,0},{2,1},{3,2},{4,3},{5,4},{6,5},{7,6},{8,7},{9,8},{10,9... | collective-permute-start | bytes 786440 | tf_op jit(solution)/shard_map/ppermute | solution.py:69
  198.6 9.5 %collective-permute-start.6 = (f32[2,2,128,128]{3,2,0,1:T(8,128)S(1)}, f32[2,2,128,128]{3,2,0,1:T(8,128)S(1)}, u32[]{:S(2)}, u32[]{:S(2)}) collective-permute-start(f32[2,2,128,128]{3,2,0,1:T(8,128)S(1)} %collective-permute-done.4), channel_id=1, source_target_pairs={{0,1},{1,2},{2,3},{3,4},{4,5},{5,6},{6,7},{7,8},{8,9},{9,10},{10,1... | collective-permute-start | bytes 786440 | tf_op jit(solution)/shard_map/ppermute | solution.py:64
  201.1 47.8 %copy-start = (f32[1,2,2048,128]{3,2,1,0:T(8,128)S(1)}, f32[1,2,2048,128]{3,2,1,0:T(8,128)}, u32[]{:S(2)}) copy-start(f32[1,2,2048,128]{3,2,1,0:T(8,128)} %param.11) | copy-start | bytes 6291460
  201.8 9.0 %collective-permute-start.7 = (f32[2,2,128,128]{3,2,0,1:T(8,128)S(1)}, f32[2,2,128,128]{3,2,0,1:T(8,128)S(1)}, u32[]{:S(2)}, u32[]{:S(2)}) collective-permute-start(f32[2,2,128,128]{3,2,0,1:T(8,128)S(1)} %collective-permute-done.5), channel_id=1, source_target_pairs={{0,15},{1,0},{2,1},{3,2},{4,3},{5,4},{6,5},{7,6},{8,7},{9,8},{10,9... | collective-permute-start | bytes 786440 | tf_op jit(solution)/shard_map/ppermute | solution.py:69
  208.1 10.3 %collective-permute-start.8 = (f32[2,2,128,128]{3,2,0,1:T(8,128)S(1)}, f32[2,2,128,128]{3,2,0,1:T(8,128)S(1)}, u32[]{:S(2)}, u32[]{:S(2)}) collective-permute-start(f32[2,2,128,128]{3,2,0,1:T(8,128)S(1)} %collective-permute-done.6), channel_id=1, source_target_pairs={{0,1},{1,2},{2,3},{3,4},{4,5},{5,6},{6,7},{7,8},{8,9},{9,10},{10,1... | collective-permute-start | bytes 786440 | tf_op jit(solution)/shard_map/ppermute | solution.py:64
  210.8 10.5 %collective-permute-start.9 = (f32[2,2,128,128]{3,2,0,1:T(8,128)S(1)}, f32[2,2,128,128]{3,2,0,1:T(8,128)S(1)}, u32[]{:S(2)}, u32[]{:S(2)}) collective-permute-start(f32[2,2,128,128]{3,2,0,1:T(8,128)S(1)} %collective-permute-done.7), channel_id=1, source_target_pairs={{0,15},{1,0},{2,1},{3,2},{4,3},{5,4},{6,5},{7,6},{8,7},{9,8},{10,9... | collective-permute-start | bytes 786440 | tf_op jit(solution)/shard_map/ppermute | solution.py:69
  218.4 11.5 %collective-permute-start.10 = (f32[2,2,128,128]{3,2,0,1:T(8,128)S(1)}, f32[2,2,128,128]{3,2,0,1:T(8,128)S(1)}, u32[]{:S(2)}, u32[]{:S(2)}) collective-permute-start(f32[2,2,128,128]{3,2,0,1:T(8,128)S(1)} %collective-permute-done.8), channel_id=1, source_target_pairs={{0,1},{1,2},{2,3},{3,4},{4,5},{5,6},{6,7},{7,8},{8,9},{9,10},{10,1... | collective-permute-start | bytes 786440 | tf_op jit(solution)/shard_map/ppermute | solution.py:64
  221.4 10.5 %collective-permute-start.11 = (f32[2,2,128,128]{3,2,0,1:T(8,128)S(1)}, f32[2,2,128,128]{3,2,0,1:T(8,128)S(1)}, u32[]{:S(2)}, u32[]{:S(2)}) collective-permute-start(f32[2,2,128,128]{3,2,0,1:T(8,128)S(1)} %collective-permute-done.9), channel_id=1, source_target_pairs={{0,15},{1,0},{2,1},{3,2},{4,3},{5,4},{6,5},{7,6},{8,7},{9,8},{10,9... | collective-permute-start | bytes 786440 | tf_op jit(solution)/shard_map/ppermute | solution.py:69
  229.8 9.5 %collective-permute-start.12 = (f32[2,2,128,128]{3,2,0,1:T(8,128)S(1)}, f32[2,2,128,128]{3,2,0,1:T(8,128)S(1)}, u32[]{:S(2)}, u32[]{:S(2)}) collective-permute-start(f32[2,2,128,128]{3,2,0,1:T(8,128)S(1)} %collective-permute-done.10), channel_id=1, source_target_pairs={{0,1},{1,2},{2,3},{3,4},{4,5},{5,6},{6,7},{7,8},{8,9},{9,10},{10,1... | collective-permute-start | bytes 786440 | tf_op jit(solution)/shard_map/ppermute | solution.py:64
  231.8 9.6 %collective-permute-start.13 = (f32[2,2,128,128]{3,2,0,1:T(8,128)S(1)}, f32[2,2,128,128]{3,2,0,1:T(8,128)S(1)}, u32[]{:S(2)}, u32[]{:S(2)}) collective-permute-start(f32[2,2,128,128]{3,2,0,1:T(8,128)S(1)} %collective-permute-done.11), channel_id=1, source_target_pairs={{0,15},{1,0},{2,1},{3,2},{4,3},{5,4},{6,5},{7,6},{8,7},{9,8},{10,9... | collective-permute-start | bytes 786440 | tf_op jit(solution)/shard_map/ppermute | solution.py:69
  239.3 9.5 %collective-permute-start.14 = (f32[2,2,128,128]{3,2,0,1:T(8,128)S(1)}, f32[2,2,128,128]{3,2,0,1:T(8,128)S(1)}, u32[]{:S(2)}, u32[]{:S(2)}) collective-permute-start(f32[2,2,128,128]{3,2,0,1:T(8,128)S(1)} %collective-permute-done.12), channel_id=1, source_target_pairs={{0,1},{1,2},{2,3},{3,4},{4,5},{5,6},{6,7},{7,8},{8,9},{9,10},{10,1... | collective-permute-start | bytes 786440 | tf_op jit(solution)/shard_map/ppermute | solution.py:64
Sparse Core Ops, SparseCore 0:
  11.7 63.0 all-gather.1
  88.8 80.2 reduce-scatter.1
